TPU v7x, 32 devices: a whole 2x2x4 slice. The times are simulated.
32 devices in a mesh: parts: 2 (over y), blk: 4 (over z), dim: 2 (over x), qs: 2 (over core).
Axes of the slice: x: 2, y: 2, z: 4, core: 2. Of those that a mesh axis runs over, the one named last changes fastest.
Arguments:
- train_grads: bfloat16 [1024, 65536], P(('parts', 'blk'), 'dim'), parts along dimension 0, may hold values from -6 to 6
- query_grads: bfloat16 [1024, 65536], P(('parts', 'blk', 'qs'), 'dim'), parts along dimension 0, may hold values from -0.0078125 to 0.0078125
- fisher: float32 [65536], P('dim'), may hold values from 0.05 to 5
- train_ids: int32 [1024], P(('parts', 'blk', 'dim')), parts along dimension 0, may hold values from 0 to 15
- query_ids: int32 [1024], P('parts'), parts along dimension 0, may hold values from 0 to 15
Outputs:
- scores: float32 [1024, 256], P(('parts', 'blk', 'dim'), 'qs'), parts along dimension 0
There are 2 independent parts, one for each index of `parts`. A program takes and returns all parts, laid end to end along the dimension named above; an argument that names none is the same for every part. Nothing has to cross between parts.
All inputs are finite; a program needn't handle non-finite values.
Results may differ from a plain program's by a relative error of at most 0.0029.
Values may be sent and summed in bfloat16 or wider, within the bound.
A program may use at most 64 MiB of HBM per device.

v0:
```python
import jax
import jax.numpy as jnp
from jax import lax
from jax.sharding import PartitionSpec as P

STEPS = 2


damping = 0.1


def from_behind(block, axis, distance):
    devices = range(lax.axis_size(axis))
    route = [((i - distance) % len(devices), i) for i in devices]
    return lax.ppermute(block, axis, route)


def score_tile(train_rows, query_rows):
    return jnp.einsum("tk,qk->tq", train_rows, query_rows, preferred_element_type=jnp.float32)


def on_device(train_grads, query_grads, fisher, train_ids, query_ids):
    scaled = (query_grads.astype(jnp.float32) / (fisher + damping)).astype(jnp.bfloat16)
    cycle_size = lax.axis_size("blk")
    half_count = lax.axis_size("qs")
    cycle_index = lax.axis_index("blk")
    half_index = lax.axis_index("qs")
    query_count = scaled.shape[0]
    partials = []
    current = scaled
    for offset in range(STEPS):
        if offset > 0:
            current = from_behind(current, "blk", 1)
        partials.append(score_tile(train_grads, current))
    reduced = jnp.concatenate(
        [
            lax.psum_scatter(partial_value, "dim", scatter_dimension=0, tiled=True)
            for partial_value in partials
        ],
        axis=1,
    )
    key_pieces = []
    for offset in range(STEPS):
        start = ((cycle_index - offset) % cycle_size * half_count + half_index) * query_count
        key_pieces.append(lax.dynamic_slice_in_dim(query_ids, start, query_count, 0))
    window_keys = jnp.concatenate(key_pieces)
    return jnp.where(train_ids[:, None] == window_keys[None, :], jnp.zeros_like(reduced), reduced)


def solution(mesh):
    return jax.shard_map(
        on_device,
        mesh=mesh,
        in_specs=(
            P(("parts", "blk"), "dim"),
            P(("parts", "blk", "qs"), "dim"),
            P("dim"),
            P(("parts", "blk", "dim")),
            P("parts"),
        ),
        out_specs=P(("parts", "blk", "dim"), "qs"),
        check_vma=False,
    )
```

profile of v0, /device:TPU:0, one launch (start us, length us, event | category | flops | bytes accessed | tf_op | source)
XLA Modules:
  0.0 134.9 jit_solution(18257133639236476413)
XLA Ops:
  6.5 0.0 reduce-scatter.7.cloned.1.call-start
  6.5 0.9 broadcast_add_fusion
  7.5 0.0 copy-start
  7.5 5.1 %divide_convert_fusion = bf16[64,32768]{1,0:T(8,128)(2,1)} fusion(bf16[64,32768]{1,0:T(8,128)(2,1)} %param.6, f32[32768]{0:T(1024)S(1)} %broadcast_add_fusion), kind=kLoop, calls=%fused_computation | loop fusion | flops 6291456 | bytes 8519680 | tf_op jit(solution)/shard_map/convert_element_type | solution.py:23
  12.6 0.0 copy-start.2
  12.6 3.0 %collective-permute-start = (bf16[64,32768]{1,0:T(8,128)(2,1)}, bf16[64,32768]{1,0:T(8,128)(2,1)}, u32[]{:S(2)}, u32[]{:S(2)}) collective-permute-start(bf16[64,32768]{1,0:T(8,128)(2,1)} %divide_convert_fusion), channel_id=1, source_target_pairs={{12,0},{0,4},{4,8},{8,12},{13,1},{1,5},{5,9},{9,13},{14,2},{2,6},{... | collective-permute-start | bytes 12582920 | tf_op jit(solution)/shard_map/ppermute | solution.py:15
  15.6 0.0 copy-done
  15.6 5.2 %convolution_bitcast_fusion.1 = f32[128,64]{0,1:T(8,128)S(1)} fusion(bf16[64,32768]{1,0:T(8,128)(2,1)} %divide_convert_fusion, bf16[128,32768]{1,0:T(8,128)(2,1)S(1)} %copy-done), kind=kOutput, calls=%fused_computation.2 | convolution fusion | flops 536870912 | bytes 12615680 | tf_op jit(solution)/shard_map/tk,qk->tq/dot_general | solution.py:19
  20.9 0.7 copy.8
  21.6 0.0 reduce-scatter.7.cloned.1.call-update
  21.6 0.0 reduce-scatter.9.cloned.1.call-start
  21.7 0.0 copy-done.2
  21.7 0.1 fusion
  21.8 86.7 %collective-permute-done = bf16[64,32768]{1,0:T(8,128)(2,1)} collective-permute-done((bf16[64,32768]{1,0:T(8,128)(2,1)}, bf16[64,32768]{1,0:T(8,128)(2,1)}, u32[]{:S(2)}, u32[]{:S(2)}) %collective-permute-start) | collective-permute-done | bytes 4194336 | tf_op jit(solution)/shard_map/ppermute | solution.py:15
  108.5 7.7 %convolution_bitcast_fusion = f32[128,64]{0,1:T(8,128)S(1)} fusion(bf16[64,32768]{1,0:T(8,128)(2,1)} %collective-permute-done, bf16[128,32768]{1,0:T(8,128)(2,1)} %param.5), kind=kOutput, calls=%fused_computation.1 | convolution fusion | flops 536870912 | bytes 12615680 | tf_op jit(solution)/shard_map/tk,qk->tq/dot_general | solution.py:19
  116.2 0.7 copy.10
  116.9 0.0 reduce-scatter.9.cloned.1.call-update
  117.0 0.1 pad_add_fusion
  117.0 0.8 copy.9
  117.9 8.6 %reduce-scatter.9.cloned.1.call-done = f32[64,64]{1,0:T(8,128)} async-done(((f32[128,64]{1,0:T(8,128)}), f32[64,64]{1,0:T(8,128)}) %reduce-scatter.9.cloned.1.call-update) | async-done | bytes 16400
  126.4 0.8 copy.11
  127.3 0.0 copy-done.1
  127.3 0.1 maximum_select_fusion
  127.4 0.7 copy.7
  (2 shorter events, 0.0 us)
Async XLA Ops:
  6.5 110.5 %reduce-scatter.7.cloned.1.call-start = ((), (), s32[]{:S(2)}) async-start(), calls=%async_computation.2 | async-start | bytes 98304
  7.5 8.2 %copy-start = (bf16[128,32768]{1,0:T(8,128)(2,1)S(1)}, bf16[128,32768]{1,0:T(8,128)(2,1)}, u32[]{:S(2)}) copy-start(bf16[128,32768]{1,0:T(8,128)(2,1)} %param.5) | copy-start | bytes 25165828
  12.6 9.1 %copy-start.2 = (s32[512]{0:T(512)S(1)}, s32[512]{0:T(512)}, u32[]{:S(2)}) copy-start(s32[512]{0:T(512)} %param.9) | copy-start | bytes 6148
  12.6 95.9 %collective-permute-start = (bf16[64,32768]{1,0:T(8,128)(2,1)}, bf16[64,32768]{1,0:T(8,128)(2,1)}, u32[]{:S(2)}, u32[]{:S(2)}) collective-permute-start(bf16[64,32768]{1,0:T(8,128)(2,1)} %divide_convert_fusion), channel_id=1, source_target_pairs={{12,0},{0,4},{4,8},{8,12},{13,1},{1,5},{5,9},{9,13},{14,2},{2,6},{... | collective-permute-start | bytes 12582920 | tf_op jit(solution)/shard_map/ppermute | solution.py:15
  21.6 104.8 %reduce-scatter.9.cloned.1.call-start = ((), (), s32[]{:S(2)}) async-start(), calls=%async_computation.3 | async-start | bytes 98304
  21.8 105.5 %copy-start.1 = (s32[64]{0:T(128)S(1)}, s32[64]{0:T(128)}, u32[]{:S(2)}) copy-start(s32[64]{0:T(128)} %param.8) | copy-start | bytes 772
Sparse Core Ops, SparseCore 0:
  21.7 10.2 reduce-scatter.6
  117.1 9.3 reduce-scatter.8
where the time goes:
time: 135 us
  waiting for transfers between devices  95.3 us (71%)
  between operations  13.5 us (10%)
  matrix products  12.9 us (10%)
  other arithmetic  6.21 us (5%)
  local copies, waits for them, and re-layouts  3.89 us (3%)
  starting transfers between devices  3.07 us (2%)
    ppermute x1, waiting for transfers between devices, from_behind(): return lax.ppermute(block, axis, route)  86.7 us
    dot_general x2, matrix products, score_tile(): jnp.einsum('tk,qk->tq', train_rows, query_rows, preferred_element_type=jn...  12.9 us
    unnamed x4, waiting for transfers between devices  8.61 us
    convert_element_type x1, other arithmetic, on_device(): (query_grads.astype(jnp.float32) / (fisher + damping)).astype(jnp.bfloat16)  5.14 us
    unnamed x10, local copies, waits for them, and re-layouts  3.11 us
    ppermute x1, starting transfers between devices, from_behind(): return lax.ppermute(block, axis, route)  3.02 us
  transfers between devices with their start and end apart: 3, of which 2 were waited for; matrix products, arithmetic and copies ran while one was open for 11% of the time, Pallas kernels for 0%

commit v1 on v0

v1 whole, which is shorter than its diff:
```python
import functools

import jax
import jax.numpy as jnp
from jax import lax
from jax.experimental import pallas as pl
from jax.experimental.pallas import tpu as pltpu
from jax.sharding import PartitionSpec as P

STEPS = 2
DAMPING = 0.1
CHUNK = 2048
IN_FLIGHT = 4
MESH = pl.DeviceIdType.MESH


def kernel(sizes, train_hbm, query_hbm, fisher_hbm, train_ids_hbm, query_ids_hbm, out_ref,
           train, own, inbox, scale, train_ids, query_ids, partial, peers,
           send_sem, recv_sem, load_sem, peer_send_sem, peer_recv_sem):
    cycle, dims, halves = sizes
    blk = lax.axis_index("blk")
    dim = lax.axis_index("dim")
    half = lax.axis_index("qs")
    after = lax.rem(blk + 1, cycle)
    before = lax.rem(blk + cycle - 1, cycle)
    train_rows = train.shape[0]
    query_rows, depth = own.shape
    owned = train_rows // dims
    chunks = depth // CHUNK

    def peer(k):
        return lax.rem(dim + k, dims)

    barrier = pltpu.get_barrier_semaphore()
    pl.semaphore_signal(barrier, inc=1, device_id={"blk": before}, device_id_type=MESH)
    for k in range(1, dims):
        pl.semaphore_signal(barrier, inc=1, device_id={"dim": peer(k)}, device_id_type=MESH)
    pl.semaphore_wait(barrier, dims)

    def transfer(i):
        return pltpu.make_async_remote_copy(
            src_ref=query_hbm.at[:, pl.ds(pl.multiple_of(i * CHUNK, CHUNK), CHUNK)],
            dst_ref=inbox.at[i],
            send_sem=send_sem.at[i],
            recv_sem=recv_sem.at[i],
            device_id={"blk": after},
            device_id_type=MESH,
        )

    flight = min(IN_FLIGHT, chunks)
    for i in range(flight):
        transfer(i).start()

    loads = [
        pltpu.make_async_copy(source, target, load_sem.at[n])
        for n, (source, target) in enumerate([
            (fisher_hbm, scale), (query_hbm, own), (train_hbm, train),
            (train_ids_hbm, train_ids), (query_ids_hbm, query_ids)])
    ]
    for load in loads:
        load.start()
    for load in loads:
        load.wait()

    scale[...] = 1.0 / (scale[...] + DAMPING)

    def score(columns, rows, total):
        scaled = (rows.astype(jnp.float32) * scale[:, columns]).astype(jnp.bfloat16)
        return total + lax.dot_general(
            train[:, columns], scaled, (((1,), (1,)), ((), ())), preferred_element_type=jnp.float32)

    def columns_of(i):
        return pl.ds(pl.multiple_of(i * CHUNK, CHUNK), CHUNK)

    zero = jnp.zeros((train_rows, query_rows), jnp.float32)

    def own_step(i, total):
        columns = columns_of(i)
        return score(columns, own[:, columns], total)

    def exchange(step):
        copies = []
        for k in range(1, dims):
            copies.append(pltpu.make_async_remote_copy(
                src_ref=partial.at[step, pl.ds(pl.multiple_of(peer(k) * owned, owned), owned)],
                dst_ref=peers.at[step, k - 1],
                send_sem=peer_send_sem.at[step, k - 1],
                recv_sem=peer_recv_sem.at[step, k - 1],
                device_id={"dim": peer(k)},
                device_id_type=MESH,
            ))
        for copy in copies:
            copy.start()
        return copies

    partial[0] = lax.fori_loop(0, chunks, own_step, zero)
    first = exchange(0)

    def same_cluster():
        row = train_ids[...].astype(jnp.float32)
        diagonal = (lax.broadcasted_iota(jnp.int32, (owned, owned), 0)
                    == lax.broadcasted_iota(jnp.int32, (owned, owned), 1))
        column = jnp.sum(jnp.where(diagonal, jnp.broadcast_to(row, (owned, owned)), 0.0), axis=1, keepdims=True)
        equal = []
        for step in range(STEPS):
            group = halves * query_rows
            source = lax.rem(blk + cycle - step, cycle)
            both = query_ids[:, pl.ds(pl.multiple_of(source * group, group), group)].astype(jnp.float32)
            keys = both[:, :query_rows]
            for h in range(1, halves):
                keys = jnp.where(half == h, both[:, h * query_rows:(h + 1) * query_rows], keys)
            equal.append(jnp.broadcast_to(column, (owned, query_rows)) == jnp.broadcast_to(keys, (owned, query_rows)))
        return equal

    equal = same_cluster()
    mine = pl.ds(pl.multiple_of(dim * owned, owned), owned)

    def finish(step, copies):
        total = partial[step, mine]
        for k, copy in enumerate(copies):
            copy.wait_recv()
            total = total + peers[step, k]
        out_ref[:, step * query_rows:(step + 1) * query_rows] = jnp.where(equal[step], 0.0, total)

    finish(0, first)

    def next_step(i, total):
        transfer(i).wait_send()

        @pl.when(i + flight < chunks)
        def _():
            transfer(i + flight).start()

        transfer(i).wait_recv()
        return score(columns_of(i), inbox[i], total)

    partial[1] = lax.fori_loop(0, chunks, next_step, zero)
    second = exchange(1)
    finish(1, second)
    for copy in first + second:
        copy.wait_send()


def solution(mesh):
    sizes = (mesh.shape["blk"], mesh.shape["dim"], mesh.shape["qs"])
    dims = sizes[1]

    def on_device(train_grads, query_grads, fisher, train_ids, query_ids):
        train_rows, depth = train_grads.shape
        query_rows = query_grads.shape[0]
        owned = train_ids.shape[0]
        chunks = depth // CHUNK
        out_shape = jax.ShapeDtypeStruct((owned, STEPS * query_rows), jnp.float32)
        return pl.pallas_call(
            functools.partial(kernel, sizes),
            out_shape=out_shape,
            in_specs=[pl.BlockSpec(memory_space=pltpu.HBM)] * 5,
            out_specs=pl.BlockSpec(memory_space=pltpu.VMEM),
            scratch_shapes=[
                pltpu.VMEM((train_rows, depth), train_grads.dtype),
                pltpu.VMEM((query_rows, depth), query_grads.dtype),
                pltpu.VMEM((chunks, query_rows, CHUNK), query_grads.dtype),
                pltpu.VMEM((1, depth), jnp.float32),
                pltpu.VMEM((1, owned), jnp.int32),
                pltpu.VMEM((1, query_ids.shape[0]), jnp.int32),
                pltpu.VMEM((STEPS, train_rows, query_rows), jnp.float32),
                pltpu.VMEM((STEPS, max(dims - 1, 1), owned, query_rows), jnp.float32),
                pltpu.SemaphoreType.DMA((chunks,)),
                pltpu.SemaphoreType.DMA((chunks,)),
                pltpu.SemaphoreType.DMA((5,)),
                pltpu.SemaphoreType.DMA((STEPS, max(dims - 1, 1))),
                pltpu.SemaphoreType.DMA((STEPS, max(dims - 1, 1))),
            ],
            cost_estimate=pl.CostEstimate(
                flops=4 * train_rows * query_rows * depth,
                bytes_accessed=2 * depth * (train_rows + 2 * query_rows), transcendentals=0),
            compiler_params=pltpu.CompilerParams(
                collective_id=0, has_side_effects=True, vmem_limit_bytes=48 << 20),
        )(train_grads, query_grads, fisher.reshape(1, -1), train_ids.reshape(1, -1), query_ids.reshape(1, -1))

    return jax.shard_map(
        on_device,
        mesh=mesh,
        in_specs=(
            P(("parts", "blk"), "dim"),
            P(("parts", "blk", "qs"), "dim"),
            P("dim"),
            P(("parts", "blk", "dim")),
            P("parts"),
        ),
        out_specs=P(("parts", "blk", "dim"), "qs"),
        check_vma=False,
    )
```

time: 135 us -> 105 us (0.78)
  Pallas kernels: 0 us -> 100 us
  waiting for transfers between devices: 95.3 us -> 0 us
  between operations: 13.5 us -> 0.01 us
  matrix products: 12.9 us -> 0 us
  other arithmetic: 6.21 us -> 0 us
  starting transfers between devices: 3.07 us -> 0 us
    pallas_call x0 -> x1, Pallas kernels: none -> 100 us  [on_device(): pl.pallas_call(functools.partial(kernel, sizes), out_shape=out_shape, in_...]
    ppermute x1 -> x0, waiting for transfers between devices: 86.7 us -> none  [from_behind(): return lax.ppermute(block, axis, route)]
    dot_general x2 -> x0, matrix products: 12.9 us -> none  [score_tile(): jnp.einsum('tk,qk->tq', train_rows, query_rows, preferred_element_type=jn...]
    unnamed x4 -> x0, waiting for transfers between devices: 8.61 us -> none
    convert_element_type x1 -> x0, other arithmetic: 5.14 us -> none  [on_device(): (query_grads.astype(jnp.float32) / (fisher + damping)).astype(jnp.bfloat16)]
    ppermute x1 -> x0, starting transfers between devices: 3.02 us -> none  [from_behind(): return lax.ppermute(block, axis, route)]
    unnamed x10 -> x9, local copies, waits for them, and re-layouts: 3.11 us -> 5.04 us
  transfers between devices with their start and end apart: 3 -> 0, of which waited for: 2 -> 0; matrix products, arithmetic and copies ran while one was open for 11% -> 0% of each run, Pallas kernels for 0% -> 0%
where the time goes in v1:
time: 105 us
  Pallas kernels  100 us (95%)
  local copies, waits for them, and re-layouts  5.04 us (5%)
    pallas_call x1, Pallas kernels, on_device(): pl.pallas_call(functools.partial(kernel, sizes), out_shape=out_shape, in_...  100 us
    unnamed x9, local copies, waits for them, and re-layouts  5.04 us

profile of v1, /device:TPU:0, one launch (start us, length us, event | category | flops | bytes accessed | tf_op | source)
XLA Modules:
  0.0 105.1 jit_solution(1325052833493831161)
XLA Ops:
  0.0 0.0 copy-start
  0.0 2.2 %copy-done = bf16[64,32768]{1,0:T(8,128)(2,1)S(1)} copy-done((bf16[64,32768]{1,0:T(8,128)(2,1)S(1)}, bf16[64,32768]{1,0:T(8,128)(2,1)}, u32[]{:S(2)}) %copy-start) | copy-done | bytes 4194328
  2.2 0.0 copy-start.1
  2.2 0.9 copy-done.1
  3.1 0.0 copy-start.2
  3.1 0.7 copy-done.2
  3.8 0.0 copy-start.3
  3.8 0.7 copy-done.3
  4.4 100.0 %shard_map.55 = f32[64,128]{1,0:T(8,128)S(1)} custom-call(bf16[128,32768]{1,0:T(8,128)(2,1)} %train_hbm.1, bf16[64,32768]{1,0:T(8,128)(2,1)S(1)} %copy-done, f32[1,32768]{1,0:T(1,128)S(1)} %bitcast.3, s32[1,64]{1,0:T(1,128)S(1)} %bitcast.5, s32[1,512]{1,0:T(1,128)S(1)} %bitcast.4), custom_call_target="tpu_custom_call" | custom-call | flops 1073741824 | bytes 16777216 | tf_op jit(solution)/shard_map/pallas_call | solution.py:154
  104.4 0.6 copy.7
Async XLA Ops:
  0.0 2.2 %copy-start = (bf16[64,32768]{1,0:T(8,128)(2,1)S(1)}, bf16[64,32768]{1,0:T(8,128)(2,1)}, u32[]{:S(2)}) copy-start(bf16[64,32768]{1,0:T(8,128)(2,1)} %query_hbm.1) | copy-start | bytes 12582916
  2.2 0.9 copy-start.1
  3.1 0.7 copy-start.2
  3.8 0.7 copy-start.3

commit v2 on v1

--- a/solution.py
+++ b/solution.py
@@ -175,7 +175,7 @@
                 flops=4 * train_rows * query_rows * depth,
                 bytes_accessed=2 * depth * (train_rows + 2 * query_rows), transcendentals=0),
             compiler_params=pltpu.CompilerParams(
-                collective_id=0, has_side_effects=True, vmem_limit_bytes=48 << 20),
+                collective_id=0, has_side_effects=True, vmem_limit_bytes=60 << 20),
         )(train_grads, query_grads, fisher.reshape(1, -1), train_ids.reshape(1, -1), query_ids.reshape(1, -1))
 
     return jax.shard_map(

time: 105 us -> 102 us (0.971)
  local copies, waits for them, and re-layouts: 5.04 us -> 1.38 us
    unnamed x9 -> x1, local copies, waits for them, and re-layouts: 5.04 us -> 1.38 us
where the time goes in v2:
time: 102 us
  Pallas kernels  101 us (99%)
  local copies, waits for them, and re-layouts  1.38 us (1%)
    pallas_call x1, Pallas kernels, on_device(): pl.pallas_call(functools.partial(kernel, sizes), out_shape=out_shape, in_...  101 us

profile of v2, /device:TPU:0, one launch (start us, length us, event | category | flops | bytes accessed | tf_op | source)
XLA Modules:
  0.0 102.2 jit_solution(14725064403012414997)
XLA Ops:
  0.0 100.8 %shard_map.55 = f32[64,128]{1,0:T(8,128)} custom-call(bf16[128,32768]{1,0:T(8,128)(2,1)} %train_hbm.1, bf16[64,32768]{1,0:T(8,128)(2,1)} %query_hbm.1, f32[1,32768]{1,0:T(1,128)} %bitcast.3, s32[1,64]{1,0:T(1,128)} %bitcast.5, s32[1,512]{1,0:T(1,128)} %bitcast.4), custom_call_target="tpu_custom_call" | custom-call | flops 1073741824 | bytes 16777216 | tf_op jit(solution)/shard_map/pallas_call | solution.py:154
  100.8 1.4 %copy.7 = f32[64,128]{1,0:T(8,128)} copy(f32[64,128]{1,0:T(8,128)} %shard_map.55) | data formatting | bytes 65536

commit v3 on v1

--- a/solution.py
+++ b/solution.py
@@ -150,7 +150,12 @@
         query_rows = query_grads.shape[0]
         owned = train_ids.shape[0]
         chunks = depth // CHUNK
-        out_shape = jax.ShapeDtypeStruct((owned, STEPS * query_rows), jnp.float32)
+        out_shape = pltpu.VMEM((owned, STEPS * query_rows), jnp.float32)
+        operands = [
+            pltpu.with_memory_space_constraint(operand, pltpu.HBM)
+            for operand in (train_grads, query_grads, fisher.reshape(1, -1),
+                            train_ids.reshape(1, -1), query_ids.reshape(1, -1))
+        ]
         return pl.pallas_call(
             functools.partial(kernel, sizes),
             out_shape=out_shape,
@@ -176,7 +181,7 @@
                 bytes_accessed=2 * depth * (train_rows + 2 * query_rows), transcendentals=0),
             compiler_params=pltpu.CompilerParams(
                 collective_id=0, has_side_effects=True, vmem_limit_bytes=48 << 20),
-        )(train_grads, query_grads, fisher.reshape(1, -1), train_ids.reshape(1, -1), query_ids.reshape(1, -1))
+        )(*operands)
 
     return jax.shard_map(
         on_device,

time: 105 us -> 101 us (0.962)
  local copies, waits for them, and re-layouts: 5.04 us -> 0.62 us
    unnamed x9 -> x1, local copies, waits for them, and re-layouts: 5.04 us -> 0.62 us
where the time goes in v3:
time: 101 us
  Pallas kernels  100 us (99%)
    pallas_call x1, Pallas kernels, on_device(): pl.pallas_call(functools.partial(kernel, sizes), out_shape=out_shape, in_...  100 us

profile of v3, /device:TPU:0, one launch (start us, length us, event | category | flops | bytes accessed | tf_op | source)
XLA Modules:
  0.0 100.8 jit_solution(15464535384260041115)
XLA Ops:
  0.0 100.2 %shard_map.55 = f32[64,128]{1,0:T(8,128)S(1)} custom-call(bf16[128,32768]{1,0:T(8,128)(2,1)} %train_hbm.1, bf16[64,32768]{1,0:T(8,128)(2,1)} %query_hbm.1, f32[1,32768]{1,0:T(1,128)} %bitcast.3, s32[1,64]{1,0:T(1,128)} %bitcast.5, s32[1,512]{1,0:T(1,128)} %bitcast.4), custom_call_target="tpu_custom_call" | custom-call | flops 1073741824 | bytes 16777216 | tf_op jit(solution)/shard_map/pallas_call | solution.py:159
  100.2 0.6 copy.7

commit v4 on v3

--- a/solution.py
+++ b/solution.py
@@ -10,7 +10,7 @@
 STEPS = 2
 DAMPING = 0.1
 CHUNK = 2048
-IN_FLIGHT = 4
+NARROW = 2
 MESH = pl.DeviceIdType.MESH
 
 
@@ -47,9 +47,15 @@
             device_id_type=MESH,
         )
 
-    flight = min(IN_FLIGHT, chunks)
-    for i in range(flight):
+    narrow = min(NARROW, chunks)
+    flight = jnp.where(half == 0, chunks, narrow)
+    for i in range(narrow):
         transfer(i).start()
+
+    @pl.when(half == 0)
+    def _():
+        for i in range(narrow, chunks):
+            transfer(i).start()
 
     loads = [
         pltpu.make_async_copy(source, target, load_sem.at[n])

time: 101 us -> 99.8 us (0.988)
    pallas_call x1, Pallas kernels: 100 us -> 99 us  [on_device(): pl.pallas_call(functools.partial(kernel, sizes), out_shape=out_shape, in_...]
where the time goes in v4:
time: 99.8 us; the launch traced here: 99.7 us
  Pallas kernels  99 us (99%)
    pallas_call x1, Pallas kernels, on_device(): pl.pallas_call(functools.partial(kernel, sizes), out_shape=out_shape, in_...  99 us

profile of v4, /device:TPU:0, one launch (start us, length us, event | category | flops | bytes accessed | tf_op | source)
XLA Modules:
  0.0 99.7 jit_solution(9000220291218163706)
XLA Ops:
  0.0 99.0 %shard_map.55 = f32[64,128]{1,0:T(8,128)S(1)} custom-call(bf16[128,32768]{1,0:T(8,128)(2,1)} %train_hbm.1, bf16[64,32768]{1,0:T(8,128)(2,1)} %query_hbm.1, f32[1,32768]{1,0:T(1,128)} %bitcast.3, s32[1,64]{1,0:T(1,128)} %bitcast.5, s32[1,512]{1,0:T(1,128)} %bitcast.4), custom_call_target="tpu_custom_call" | custom-call | flops 1073741824 | bytes 16777216 | tf_op jit(solution)/shard_map/pallas_call | solution.py:165
  99.1 0.6 copy.7

commit v5 on v4

--- a/solution.py
+++ b/solution.py
@@ -9,8 +9,8 @@
 
 STEPS = 2
 DAMPING = 0.1
-CHUNK = 2048
-NARROW = 2
+CHUNK = 4096
+NARROW = 1
 MESH = pl.DeviceIdType.MESH
 
 

time: 99.8 us -> 99.5 us (level)
  the two profiles are of different devices: /device:TPU:0 before, /device:TPU:1 now
where the time goes in v5:
time: 99.5 us; the launch traced here: 99.3 us
  Pallas kernels  98.7 us (99%)
    pallas_call x1, Pallas kernels, on_device(): pl.pallas_call(functools.partial(kernel, sizes), out_shape=out_shape, in_...  98.7 us

profile of v5, /device:TPU:1, one launch (start us, length us, event | category | flops | bytes accessed | tf_op | source)
XLA Modules:
  0.0 99.3 jit_solution(5135198171707287261)
XLA Ops:
  0.0 98.7 %shard_map.55 = f32[64,128]{1,0:T(8,128)S(1)} custom-call(bf16[128,32768]{1,0:T(8,128)(2,1)} %train_hbm.1, bf16[64,32768]{1,0:T(8,128)(2,1)} %query_hbm.1, f32[1,32768]{1,0:T(1,128)} %bitcast.3, s32[1,64]{1,0:T(1,128)} %bitcast.5, s32[1,512]{1,0:T(1,128)} %bitcast.4), custom_call_target="tpu_custom_call" | custom-call | flops 1073741824 | bytes 16777216 | tf_op jit(solution)/shard_map/pallas_call | solution.py:165
  98.7 0.6 copy.7
